TPU v7x, 128 devices: a whole 4x4x4 slice. The times are simulated.
128 devices in a mesh: island: 8 (over y, core), fsdp: 16 (over z, x).
Axes of the slice: x: 4, y: 4, z: 4, core: 2. Of those that a mesh axis runs over, the one named last changes fastest.
Arguments:
- delta: bfloat16 [8, 5120, 2560], P('island', 'fsdp'), may hold values from -6 to 6
- error: bfloat16 [8, 5120, 2560], P('island', 'fsdp'), may hold values from -4 to 4
- params: float32 [5120, 2560], P('fsdp'), may hold values from -6 to 6
- momentum: float32 [5120, 2560], P('fsdp'), may hold values from -4 to 4
- q_init: float32 [2560, 64], replicated, may hold values from -6 to 6
- inputs: bfloat16 [65536, 5120], P(('island', 'fsdp')), may hold values from -0.078125 to 0.078125
Outputs:
- new_params: float32 [5120, 2560], P('fsdp')
- new_momentum: float32 [5120, 2560], P('fsdp')
- new_error: bfloat16 [8, 5120, 2560], P('island', 'fsdp')
- outputs: bfloat16 [65536, 2560], P(('island', 'fsdp'))
All inputs are finite; a program needn't handle non-finite values.
Results may differ from a plain program's by a relative error of at most 0.0049.
Values may be sent and summed in bfloat16 or wider, within the bound.
A program may use at most 128 MiB of HBM per device.

v0:
```python
import jax
import jax.numpy as jnp
from jax import lax
from jax.sharding import PartitionSpec as P


def body(delta, error, params, momentum, q_init, inputs):
    highest = lax.Precision.HIGHEST
    merged = delta[0].astype(jnp.float32) + error[0].astype(jnp.float32)
    p_local = jnp.dot(merged, q_init, precision=highest)
    p_sum = lax.psum(p_local, "island")
    gram = lax.psum(jnp.dot(p_sum.T, p_sum, precision=highest), "fsdp")
    lower = jnp.linalg.cholesky(gram)
    p_hat = jax.scipy.linalg.solve_triangular(lower, p_sum.T, lower=True).T
    q_part = jnp.dot(merged.T, p_hat, precision=highest)
    q_sum = lax.psum(q_part, ("island", "fsdp"))
    islands = lax.axis_size("island")
    approx = jnp.dot(p_hat, q_sum.T, precision=highest) / islands
    new_error = (merged - approx).astype(jnp.bfloat16)[None]
    new_momentum = 0.9 * momentum + approx
    new_params = params - 0.7 * (approx + 0.9 * new_momentum)
    weights = new_params.astype(jnp.bfloat16)
    total = jnp.dot(
        inputs,
        lax.all_gather(weights, "fsdp", axis=0, tiled=True),
        preferred_element_type=jnp.float32,
    )
    outputs = total.astype(jnp.bfloat16)
    return (new_params, new_momentum, new_error, outputs)


def solution(mesh):
    in_specs = (
        P("island", "fsdp", None),
        P("island", "fsdp", None),
        P("fsdp", None),
        P("fsdp", None),
        P(),
        P(("island", "fsdp"), None),
    )
    out_specs = (
        P("fsdp", None),
        P("fsdp", None),
        P("island", "fsdp", None),
        P(("island", "fsdp"), None),
    )
    return jax.shard_map(body, mesh=mesh, in_specs=in_specs, out_specs=out_specs, check_vma=False)
```

profile of v0, /device:TPU:1, one launch (start us, length us, event | category | flops | bytes accessed | tf_op | source)
XLA Modules:
  0.0 516.5 jit_solution(13586557282276842473)
XLA Ops:
  7.2 0.0 copy-start
  7.2 0.0 all-reduce.3.cloned.1.call-start
  7.2 1.0 copy-done
  8.3 5.6 %fusion.3 = f32[320,64]{0,1:T(8,128)} fusion(f32[2560,64]{0,1:T(8,128)S(1)} %copy-done, bf16[1,320,2560]{2,1,0:T(8,128)(2,1)} %param.7, bf16[1,320,2560]{2,1,0:T(8,128)(2,1)} %param.6), kind=kOutput, calls=%fused_computation.6 | convolution fusion | flops 631603200 | bytes 4014080 | tf_op jit(solution)/shard_map/dot_general | solution.py:10
  13.8 0.0 all-reduce.3.cloned.1.call-update
  13.9 0.0 all-reduce.5.cloned.1.call-start
  13.9 58.8 %all-reduce.3.cloned.1.call-done = f32[320,64]{0,1:T(8,128)} async-done(((f32[320,64]{0,1:T(8,128)}), f32[320,64]{0,1:T(8,128)}) %all-reduce.3.cloned.1.call-update) | async-done | bytes 81936 | tf_op jit(solution)/shard_map/psum | solution.py:11
  72.7 1.2 fusion.12
  73.9 60.3 %psum.22 = f32[64,64]{0,1:T(8,128)S(1)} all-reduce(f32[64,64]{0,1:T(8,128)S(1)} %fusion.12), channel_id=1, replica_groups=mesh['island'=8,'fsdp'=16] {'fsdp'}, use_global_device_ids=true, to_apply=%region_1.0 | all-reduce | flops 4096 | bytes 32768 | tf_op jit(solution)/shard_map/psum | solution.py:12
  134.2 0.1 copy.11
  134.3 5.8 %cholesky.16 = f32[64,64]{1,0:T(8,128)S(1)} custom-call(f32[64,64]{1,0:T(8,128)S(1)} %fusion.10), custom_call_target="Cholesky" | custom-call | tf_op jit(solution)/shard_map/jit(cholesky)/cholesky | solution.py:13
  140.2 0.6 compare_reduce_fusion
  140.8 0.7 fusion.7
  141.5 4.9 custom-call.7
  146.4 1.2 fusion.8
  147.6 8.9 %fusion.1 = f32[2560,64]{1,0:T(8,128)} fusion(f32[64,320]{1,0:T(8,128)S(1)} %fusion.8, bf16[1,320,2560]{2,1,0:T(8,128)(2,1)S(1)} %copy-done.1, bf16[1,320,2560]{2,1,0:T(8,128)(2,1)} %param.6), kind=kOutput, calls=%fused_computation.4 | convolution fusion | flops 631603200 | bytes 4014080 | tf_op jit(solution)/shard_map/dot_general | solution.py:15
  156.5 0.0 all-reduce.5.cloned.1.call-update
  156.5 0.2 all-gather.2.cloned.1.call-start
  156.7 157.7 %all-reduce.5.cloned.1.call-done = f32[2560,64]{1,0:T(8,128)} async-done(((f32[2560,64]{1,0:T(8,128)}), f32[2560,64]{1,0:T(8,128)}) %all-reduce.5.cloned.1.call-update) | async-done | bytes 655376 | tf_op jit(solution)/shard_map/psum | solution.py:16
  314.4 11.5 %fusion.11 = (bf16[320,2560]{1,0:T(8,128)(2,1)}, f32[320,2560]{1,0:T(8,128)}, f32[320,2560]{1,0:T(8,128)}, bf16[1,320,2560]{2,1,0:T(8,128)(2,1)}) fusion(f32[320,2560]{1,0:T(8,128)} %param.8, f32[320,2560]{1,0:T(8,128)} %param.9, bf16[1,320,2560]{2,1,0:T(8,128)(2,1)S(1)} %copy-done.1, bf16[1,320,2560]{2,1,0:T(8,128)(2,1)} %param.6, ...), kind=kOutput, calls=%fused_computation.23 | convolution fusion | flops 639795200 | bytes 20398080 | tf_op jit(solution)/shard_map/dot_general | solution.py:18
  325.9 0.0 all-gather.2.cloned.1.call-update
  326.0 158.1 %all-gather.2.cloned.1.call-done = bf16[5120,2560]{1,0:T(8,128)(2,1)} async-done(((bf16[320,2560]{1,0:T(8,128)(2,1)}), bf16[5120,2560]{1,0:T(8,128)(2,1)}) %all-gather.2.cloned.1.call-update) | async-done | bytes 26214416 | tf_op jit(solution)/shard_map/all_gather | solution.py:25
  484.0 21.6 %fusion = bf16[512,2560]{0,1:T(8,128)(2,1)} fusion(bf16[5120,2560]{1,0:T(8,128)(2,1)} %all-gather.2.cloned.1.call-done, bf16[512,5120]{1,0:T(8,128)(2,1)} %param.11), kind=kOutput, calls=%fused_computation.2 | convolution fusion | flops 13423083520 | bytes 34078720 | tf_op jit(solution)/shard_map/dot_general | solution.py:23
  505.6 4.4 copy.12
  (4 shorter events, 0.0 us)
Async XLA Ops:
  7.2 1.1 copy-start
  7.2 140.4 %copy-start.1 = (bf16[1,320,2560]{2,1,0:T(8,128)(2,1)S(1)}, bf16[1,320,2560]{2,1,0:T(8,128)(2,1)}, u32[]{:S(2)}) copy-start(bf16[1,320,2560]{2,1,0:T(8,128)(2,1)} %param.7) | copy-start | bytes 4915204
  7.2 65.5 %all-reduce.3.cloned.1.call-start = ((), (), s32[]{:S(2)}) async-start(), calls=%async_computation | async-start | bytes 196608 | tf_op jit(solution)/shard_map/psum | solution.py:11
  13.9 300.6 %all-reduce.5.cloned.1.call-start = ((), (), s32[]{:S(2)}) async-start(), calls=%async_computation.1 | async-start | bytes 2621440 | tf_op jit(solution)/shard_map/psum | solution.py:16
  156.5 327.5 %all-gather.2.cloned.1.call-start = ((), (), s32[]{:S(2)}) async-start(), calls=%async_computation.2 | async-start | bytes 27852800 | tf_op jit(solution)/shard_map/all_gather | solution.py:25
Sparse Core Ops, SparseCore 0:
  14.0 58.6 all-reduce.2
  156.6 157.7 all-reduce.4
  326.1 157.8 all-gather.1
where the time goes:
time: 517 us; the launch traced here: 516 us
  waiting for transfers between devices  375 us (73%)
  blocking collectives  60.3 us (12%)
  matrix products  49.9 us (10%)
  between operations  13.8 us (3%)
  other arithmetic  12.1 us (2%)
  local copies, waits for them, and re-layouts  5.48 us (1%)
    all_gather x1, waiting for transfers between devices, body(): lax.all_gather(weights, 'fsdp', axis=0, tiled=True)  158 us
    psum x1, waiting for transfers between devices, body(): q_sum = lax.psum(q_part, ('island', 'fsdp'))  158 us
    psum x1, blocking collectives, body(): gram = lax.psum(jnp.dot(p_sum.T, p_sum, precision=highest), 'fsdp')  60.3 us
    psum x1, waiting for transfers between devices, body(): p_sum = lax.psum(p_local, 'island')  58.8 us
    dot_general x1, matrix products, body(): jnp.dot(inputs, lax.all_gather(weights, 'fsdp', axis=0, tiled=True), pref...  21.6 us
    dot_general x1, matrix products, body(): approx = jnp.dot(p_hat, q_sum.T, precision=highest) / islands  11.5 us
  transfers between devices with their start and end apart: 3, of which 3 were waited for; matrix products, arithmetic and copies ran while one was open for 0% of the time, Pallas kernels for 0%

commit v1 on v0

v1 whole, which is shorter than its diff:
```python
import jax
import jax.numpy as jnp
from jax import lax
from jax.sharding import PartitionSpec as P


def body(delta, error, params, momentum, q_init, inputs):
    highest = lax.Precision.HIGHEST
    islands = lax.axis_size("island")
    base = params - 0.567 * momentum
    gathered = lax.all_gather(base.astype(jnp.bfloat16), "fsdp", axis=0, tiled=True)
    merged = delta[0].astype(jnp.float32) + error[0].astype(jnp.float32)
    p_sum = lax.psum(jnp.dot(merged, q_init, precision=highest), "island")
    p_all = lax.all_gather(p_sum, "fsdp", axis=0, tiled=True)
    raw = jnp.dot(p_sum.T, merged, precision=highest)
    raw = lax.psum(raw, ("island", "fsdp"))
    gram = jnp.dot(p_all.T, p_all, precision=highest)
    lower = jnp.linalg.cholesky(gram)
    half = jax.scipy.linalg.solve_triangular(lower, raw, lower=True)
    right = jax.scipy.linalg.solve_triangular(lower, half, lower=True, trans=1) / islands
    approx = jnp.dot(p_sum, right, precision=highest)
    new_error = (merged - approx).astype(jnp.bfloat16)[None]
    new_momentum = 0.9 * momentum + approx
    new_params = params - 0.7 * (approx + 0.9 * new_momentum)
    high = p_all.astype(jnp.bfloat16)
    low = (p_all - high.astype(jnp.float32)).astype(jnp.bfloat16)
    left = jnp.dot(inputs, jnp.concatenate([high, low], axis=1), preferred_element_type=jnp.float32)
    left = left[:, :64] + left[:, 64:]
    total = jnp.dot(inputs, gathered, preferred_element_type=jnp.float32)
    total = total - 1.33 * jnp.dot(left, right, precision=highest)
    return (new_params, new_momentum, new_error, total.astype(jnp.bfloat16))


def solution(mesh):
    in_specs = (
        P("island", "fsdp", None),
        P("island", "fsdp", None),
        P("fsdp", None),
        P("fsdp", None),
        P(),
        P(("island", "fsdp"), None),
    )
    out_specs = (
        P("fsdp", None),
        P("fsdp", None),
        P("island", "fsdp", None),
        P(("island", "fsdp"), None),
    )
    return jax.shard_map(body, mesh=mesh, in_specs=in_specs, out_specs=out_specs, check_vma=False)
```

time: 517 us -> 477 us (0.923)
  blocking collectives: 60.3 us -> 0 us
  waiting for transfers between devices: 375 us -> 386 us
  matrix products: 49.9 us -> 55.2 us
    psum x1 -> x0, blocking collectives: 60.3 us -> none  [body(): gram = lax.psum(jnp.dot(p_sum.T, p_sum, precision=highest), 'fsdp')]
    all_gather x1 -> x2, waiting for transfers between devices: 158 us -> 194 us  [the longest x1 153 us: body(): lax.all_gather(base.astype(jnp.bfloat16), 'fsdp', axis=0, tiled=True)]
    psum x2, waiting for transfers between devices: 216 us -> 192 us  [the longest x1 133 us: body(): raw = lax.psum(raw, ('island', 'fsdp'))]
    dot_general x5 -> x7, matrix products: 48.7 us -> 52.6 us  [the longest x1 21.9 us: body(): total = jnp.dot(inputs, gathered, preferred_element_type=jnp.float32)]
  transfers between devices with their start and end apart: 3 -> 4, of which waited for: 3 -> 4; matrix products, arithmetic and copies ran while one was open for 0% -> 6% of each run, Pallas kernels for 0% -> 0%
where the time goes in v1:
time: 477 us
  waiting for transfers between devices  386 us (81%)
  matrix products  55.2 us (12%)
  between operations  13.9 us (3%)
  other arithmetic  12.2 us (3%)
  local copies, waits for them, and re-layouts  9.17 us (2%)
    all_gather x1, waiting for transfers between devices, body(): lax.all_gather(base.astype(jnp.bfloat16), 'fsdp', axis=0, tiled=True)  153 us
    psum x1, waiting for transfers between devices, body(): raw = lax.psum(raw, ('island', 'fsdp'))  133 us
    psum x1, waiting for transfers between devices, body(): p_sum = lax.psum(jnp.dot(merged, q_init, precision=highest), 'island')  58.8 us
    all_gather x1, waiting for transfers between devices, body(): p_all = lax.all_gather(p_sum, 'fsdp', axis=0, tiled=True)  41 us
    dot_general x1, matrix products, body(): total = jnp.dot(inputs, gathered, preferred_element_type=jnp.float32)  21.9 us
  transfers between devices with their start and end apart: 4, of which 4 were waited for; matrix products, arithmetic and copies ran while one was open for 6% of the time, Pallas kernels for 0%

profile of v1, /device:TPU:1, one launch (start us, length us, event | category | flops | bytes accessed | tf_op | source)
XLA Modules:
  0.0 477.2 jit_solution(13373485118328698741)
XLA Ops:
  7.2 1.0 copy-done
  8.3 5.6 %fusion.3 = f32[320,64]{0,1:T(8,128)} fusion(f32[2560,64]{0,1:T(8,128)S(1)} %copy-done, bf16[1,320,2560]{2,1,0:T(8,128)(2,1)} %param.7, bf16[1,320,2560]{2,1,0:T(8,128)(2,1)} %param.6), kind=kOutput, calls=%fused_computation.6 | convolution fusion | flops 631603200 | bytes 4014080 | tf_op jit(solution)/shard_map/dot_general | solution.py:13
  13.9 58.8 %all-reduce.3.cloned.1.call-done = f32[320,64]{0,1:T(8,128)} async-done(((f32[320,64]{0,1:T(8,128)}), f32[320,64]{0,1:T(8,128)}) %all-reduce.3.cloned.1.call-update) | async-done | bytes 81936 | tf_op jit(solution)/shard_map/psum | solution.py:13
  72.8 4.8 %fusion.1 = f32[64,2560]{1,0:T(8,128)} fusion(f32[320,64]{0,1:T(8,128)} %all-reduce.3.cloned.1.call-done, bf16[1,320,2560]{2,1,0:T(8,128)(2,1)S(1)} %copy-done.2, bf16[1,320,2560]{2,1,0:T(8,128)(2,1)} %param.6), kind=kOutput, calls=%fused_computation.4 | convolution fusion | flops 631603200 | bytes 4014080 | tf_op jit(solution)/shard_map/dot_general | solution.py:15
  77.7 0.2 all-gather.4.cloned.1.call-start
  77.9 41.0 %all-gather.6.cloned.1.call-done = f32[16,320,64]{1,2,0:T(8,128)} async-done(((f32[1,320,64]{1,2,0:T(8,128)}), f32[16,320,64]{1,2,0:T(8,128)}) %all-gather.6.cloned.1.call-update) | async-done | bytes 1310736 | tf_op jit(solution)/shard_map/all_gather | solution.py:14
  118.9 3.5 copy.17
  122.3 1.8 reshape.25
  124.2 1.2 fusion.21
  125.3 0.1 copy.18
  125.4 5.8 %cholesky.16 = f32[64,64]{1,0:T(8,128)S(1)} custom-call(f32[64,64]{1,0:T(8,128)S(1)} %fusion.19), custom_call_target="Cholesky" | custom-call | tf_op jit(solution)/shard_map/jit(cholesky)/cholesky | solution.py:18
  131.3 0.6 compare_reduce_fusion
  132.0 0.7 fusion.15
  132.6 4.9 %custom-call.10 = f32[1,64,64]{1,2,0:T(8,128)S(1)} custom-call(f32[1,64,64]{2,1,0:T(8,128)S(1)} %fusion.15), custom_call_target="InvertDiagBlocksLowerTriangular" | custom-call | tf_op jit(solution)/shard_map/jit(_solve_triangular)/triangular_solve | solution.py:20
  137.5 133.3 %all-reduce.5.cloned.1.call-done = f32[64,2560]{1,0:T(8,128)} async-done(((f32[64,2560]{1,0:T(8,128)}), f32[64,2560]{1,0:T(8,128)}) %all-reduce.5.cloned.1.call-update) | async-done | bytes 655376 | tf_op jit(solution)/shard_map/psum | solution.py:16
  270.8 1.9 fusion.17
  272.8 0.7 convolution_multiply_fusion
  273.5 8.3 %multiply_subtract_fusion = (f32[320,2560]{1,0:T(8,128)}, f32[320,2560]{1,0:T(8,128)}, bf16[320,2560]{1,0:T(8,128)(2,1)}, bf16[1,320,2560]{2,1,0:T(8,128)(2,1)}) fusion(f32[320,2560]{1,0:T(8,128)} %param.8, f32[320,2560]{1,0:T(8,128)} %param.9, bf16[1,320,2560]{2,1,0:T(8,128)(2,1)S(1)} %copy-done.2, bf16[1,320,2560]{2,1,0:T(8,128)(2,1)S(1)} %copy-done.3, ...), kind=kOutput, calls=%fused_computation.10 | convolution fusion | flops 640614400 | bytes 20398080 | tf_op jit(solution)/shard_map/dot_general | solution.py:21
  281.8 0.1 subtract_convert_fusion.1
  281.9 4.4 fusion.11
  286.3 153.1 %all-gather.4.cloned.1.call-done = bf16[5120,2560]{1,0:T(8,128)(2,1)} async-done(((bf16[320,2560]{1,0:T(8,128)(2,1)}), bf16[5120,2560]{1,0:T(8,128)(2,1)}) %all-gather.4.cloned.1.call-update) | async-done | bytes 26214416 | tf_op jit(solution)/shard_map/all_gather | solution.py:11
  439.5 21.9 %fusion.22 = f32[2560,512]{1,0:T(8,128)} fusion(bf16[5120,2560]{1,0:T(8,128)(2,1)} %all-gather.4.cloned.1.call-done, bf16[512,5120]{1,0:T(8,128)(2,1)} %param.11), kind=kOutput, calls=%fused_computation.35 | convolution fusion | flops 13421772800 | bytes 36700160 | tf_op jit(solution)/shard_map/dot_general | solution.py:29
  461.4 6.4 %fusion = bf16[512,2560]{0,1:T(8,128)(2,1)S(1)} fusion(f32[2560,512]{1,0:T(8,128)} %fusion.22, f32[64,2560]{1,0:T(8,128)S(1)} %copy-done.5, f32[512,128]{0,1:T(8,128)S(1)} %fusion.11), kind=kOutput, calls=%fused_computation.1 | convolution fusion | flops 1010597888 | bytes 8781824 | tf_op jit(solution)/shard_map/dot_general | solution.py:30
  467.8 2.8 copy.20
  (22 shorter events, 0.3 us)
Async XLA Ops:
  7.2 1.1 copy-start
  7.2 65.6 %copy-start.2 = (bf16[1,320,2560]{2,1,0:T(8,128)(2,1)S(1)}, bf16[1,320,2560]{2,1,0:T(8,128)(2,1)}, u32[]{:S(2)}) copy-start(bf16[1,320,2560]{2,1,0:T(8,128)(2,1)} %param.7) | copy-start | bytes 4915204
  7.2 65.5 %all-reduce.3.cloned.1.call-start = ((), (), s32[]{:S(2)}) async-start(), calls=%async_computation | async-start | bytes 196608 | tf_op jit(solution)/shard_map/psum | solution.py:13
  13.9 105.0 %all-gather.6.cloned.1.call-start = ((), (), s32[]{:S(2)}) async-start(), calls=%async_computation.3 | async-start | bytes 1671168 | tf_op jit(solution)/shard_map/all_gather | solution.py:14
  72.7 198.1 %all-reduce.5.cloned.1.call-start = ((), (), s32[]{:S(2)}) async-start(), calls=%async_computation.1 | async-start | bytes 1310720 | tf_op jit(solution)/shard_map/psum | solution.py:16
  77.7 361.8 %all-gather.4.cloned.1.call-start = ((), (), s32[]{:S(2)}) async-start(), calls=%async_computation.2 | async-start | bytes 27852800 | tf_op jit(solution)/shard_map/all_gather | solution.py:11
  124.2 149.3 %copy-start.6 = (f32[320,64]{0,1:T(8,128)S(1)}, f32[320,64]{0,1:T(8,128)}, u32[]{:S(2)}) copy-start(f32[320,64]{0,1:T(8,128)} %all-reduce.3.cloned.1.call-done) | copy-start | bytes 245764
  270.8 2.6 copy-start.3
  273.5 8.3 %copy-start.4 = (f32[64,2560]{1,0:T(8,128)}, f32[64,2560]{1,0:T(8,128)S(1)}, u32[]{:S(2)}) copy-start(f32[64,2560]{1,0:T(8,128)S(1)} %convolution_multiply_fusion) | copy-start | bytes 1966084
  439.5 21.9 %copy-start.5 = (f32[64,2560]{1,0:T(8,128)S(1)}, f32[64,2560]{1,0:T(8,128)}, u32[]{:S(2)}) copy-start(f32[64,2560]{1,0:T(8,128)} %copy-done.4) | copy-start | bytes 1966084
  461.4 9.2 %copy-start.1 = (f32[2560,64]{0,1:T(8,128)S(1)}, f32[2560,64]{0,1:T(8,128)}, u32[]{:S(2)}) copy-start(f32[2560,64]{0,1:T(8,128)} %param.10) | copy-start | bytes 1966084
Sparse Core Ops, SparseCore 0:
  14.0 58.6 all-reduce.2
  75.1 43.7 all-gather.5
  124.9 145.9 all-reduce.4
  281.9 157.5 all-gather.3

commit v2 on v0

v2 whole, which is shorter than its diff:
```python
import jax
import jax.numpy as jnp
from jax import lax
from jax.experimental import pallas as pl
from jax.experimental.pallas import tpu as pltpu
from jax.sharding import PartitionSpec as P

BF = jnp.bfloat16
F32 = jnp.float32
MESH = pl.DeviceIdType.MESH

ROWS = 320
HALF = 1280
UNIT = 640
STREAM = 112
CROSS = 48
WIDE = 1536
ROUNDS = 15
OFFS = (0, -1, 1, 2)


def plan():
    table = [[None] * 4 for _ in range(ROUNDS)]
    for side, (h0, h1, back) in enumerate(((0, 1, -1), (1, 0, 1))):
        x, z = side, 2 + side
        table[0][x], table[1][x], table[2][x] = ("a", 0, 0, h0), ("a", 0, 0, h1), ("a", back, 0, h0)
        table[0][z], table[1][z], table[2][z] = ("b", 0, 0, h0), ("b", 0, 0, h1), ("b", 0, back, h0)
        for k, off in enumerate(OFFS):
            table[3 + 3 * k][x] = ("b", 0, off, h0)
            table[4 + 3 * k][x] = ("b", 0, off, h1)
            table[5 + 3 * k][x] = ("b", back, off, h0)
            table[3 + 2 * k][z] = ("a", off, 0, h0)
            table[4 + 2 * k][z] = ("a", off, 0, h1)
            table[11 + k][z] = ("a", off, back, h0)
    return table


TABLE = plan()
UP = [(1, -1, 0), (1, 1, 0), (2, 2, 0)]
for _k, _o in enumerate(OFFS):
    UP += [(4 + 2 * _k, _o, -1), (4 + 2 * _k, _o, 1)]
UP += [(11 + _k, _o, 2) for _k, _o in enumerate(OFFS)]
DOWN = [(1, 0, -1), (1, 0, 1), (2, 0, 2)]
for _k, _o in enumerate(OFFS):
    DOWN += [(4 + 3 * _k, -1, _o), (4 + 3 * _k, 1, _o), (5 + 3 * _k, 2, _o)]


def kernel(
    delta, error, params, momentum, q_init, inputs,
    new_params, new_momentum, new_error, outputs,
    wbuf, xin, acc, dl, er, prm, mom, q32, q2, obuf, sbuf,
    ploc, ph1, ph2, pk, p2cat, pgb, pfull, tacc, tcat,
    rloc, rin, racc, yin, s16, t16, xrs, zrs, rfull, wf, wcat,
    plane_send, plane_recv, cross_send, cross_recv, load, store,
    c_send, c_recv, in_send, in_recv, out_send, out_recv,
):
    i, f = lax.axis_index("island"), lax.axis_index("fsdp")
    y, c = i // 2, lax.rem(i, 2)
    z, x = f // 4, lax.rem(f, 4)
    parity = lax.rem(y, 2)

    def wrap(v):
        return lax.rem(v + 4, 4)

    def peer(dx=0, dy=0, dz=0, dc=0):
        return (wrap(y + dy) * 2 + lax.rem(c + dc, 2), wrap(z + dz) * 4 + wrap(x + dx))

    def shard(dx, dz):
        return wrap(z + dz) * 4 + wrap(x + dx)

    PEERS = [dict(dx=1), dict(dx=-1), dict(dx=2), dict(dy=1), dict(dy=-1), dict(dy=2),
             dict(dz=1), dict(dz=-1), dict(dz=2), dict(dc=1)]
    LINKS = [dict(dx=1), dict(dx=-1), dict(dz=1), dict(dz=-1)]

    barrier = pltpu.get_barrier_semaphore()
    for p in PEERS:
        pl.semaphore_signal(barrier, inc=1, device_id=peer(**p), device_id_type=MESH)

    def mine(col):
        return pl.ds(pl.multiple_of(col, 128), HALF)

    loads = {}

    def start_load(n, src, dst):
        loads[n] = pltpu.make_async_copy(src, dst, load.at[n])
        loads[n].start()

    start_load(0, params.at[:, mine(c * HALF)], prm.at[c])
    start_load(1, momentum.at[:, mine(c * HALF)], mom.at[c])
    start_load(2, q_init, q32)
    start_load(3, delta.at[0], dl)
    start_load(4, error.at[0], er)
    start_load(5, inputs, xin.at[c])
    start_load(6, params.at[:, mine((1 - c) * HALF)], prm.at[1 - c])
    start_load(7, momentum.at[:, mine((1 - c) * HALF)], mom.at[1 - c])

    loads[0].wait()
    loads[1].wait()

    @pl.loop(0, ROWS // 32)
    def _(t):
        r = pl.ds(pl.multiple_of(t * 32, 32), 32)
        b = prm[c, r, :] - 0.567 * mom[c, r, :]
        wbuf[pl.ds(pl.multiple_of(f * ROWS + t * 32, 32), 32), :] = b.astype(BF)

    pl.semaphore_wait(barrier, len(PEERS))

    def region(stream, dx, dz, h):
        row = shard(dx, dz) * ROWS + CROSS * parity + (0 if stream == "a" else 160)
        return wbuf.at[pl.ds(pl.multiple_of(row, 16), STREAM), pl.ds(h * UNIT, UNIT)]

    def plane_copy(r, k, arriving=False):
        stream, dx, dz, h = TABLE[r][k]
        if arriving:
            step = -1 if k % 2 == 0 else 1
            dx, dz = (dx + step, dz) if k < 2 else (dx, dz + step)
        here = region(stream, dx, dz, h)
        return pltpu.make_async_remote_copy(
            src_ref=here, dst_ref=here, send_sem=plane_send.at[r, k], recv_sem=plane_recv.at[r, k],
            device_id=peer(**LINKS[k]), device_id_type=MESH)

    def cross_copy(way, j, arriving=False):
        _, dx, dz = (UP, DOWN)[way][j]
        par = 1 - parity if arriving else parity
        row = shard(dx, dz) * ROWS + 160 * way + 112 * par
        here = wbuf.at[pl.ds(pl.multiple_of(row, 16), CROSS), :]
        return pltpu.make_async_remote_copy(
            src_ref=here, dst_ref=here, send_sem=cross_send.at[way, j], recv_sem=cross_recv.at[way, j],
            device_id=peer(dy=1 if way == 0 else -1), device_id_type=MESH)

    def issue(r):
        for k in range(4):
            plane_copy(r, k).start()

    def service(q):
        for k in range(4):
            plane_copy(q, k, arriving=True).wait_recv()
        if q + 2 < ROUNDS:
            issue(q + 2)
        for way in range(2):
            for j, (need, _, _) in enumerate((UP, DOWN)[way]):
                if need == q:
                    cross_copy(way, j).start()

    def crossed(way, *js):
        for j in js:
            cross_copy(way, j, arriving=True).wait_recv()

    issue(0)
    issue(1)

    sent = []

    def send(n, src, dst, **to):
        copy = pltpu.make_async_remote_copy(
            src_ref=src, dst_ref=dst, send_sem=c_send.at[n], recv_sem=c_recv.at[n],
            device_id=peer(**to), device_id_type=MESH)
        copy.start()
        sent.append(copy)

    def arrive(n, dst):
        pltpu.make_async_remote_copy(
            src_ref=dst, dst_ref=dst, send_sem=c_send.at[n], recv_sem=c_recv.at[n],
            device_id=peer(dc=1), device_id_type=MESH).wait_recv()

    TO = (1, -1, 2)

    def swap(v):
        return pltpu.roll(v, 64, 1)

    loads[2].wait()

    v = q32[...]
    hi = v.astype(BF)
    q2[0:64, :] = hi
    q2[64:128, :] = (v - hi.astype(F32)).astype(BF)
    loads[3].wait()
    loads[4].wait()
    last_dims = (((1,), (1,)), ((), ()))
    p_loc = lax.dot_general(dl[...], q2[...], last_dims, preferred_element_type=F32)
    p_loc = p_loc + lax.dot_general(er[...], q2[...], last_dims, preferred_element_type=F32)
    p_loc = p_loc + swap(p_loc)
    low_lane = lax.broadcasted_iota(jnp.int32, (160, 128), 1) < 64
    ploc[...] = jnp.where(low_lane, p_loc[0:160], p_loc[160:320])

    def part(ref, k):
        return ref.at[pl.ds(pl.multiple_of(k * 80, 16), 80)]

    send(0, part(ploc, 1 - c), ph1, dc=1)

    in_copies = []

    def feed(k):
        rows = xin.at[c, pl.ds(k * 128, 128)]
        copy = pltpu.make_async_remote_copy(
            src_ref=rows, dst_ref=rows, send_sem=in_send.at[k], recv_sem=in_recv.at[k],
            device_id=peer(dc=1), device_id_type=MESH)
        copy.start()
        in_copies.append(copy)

    def fed(k):
        rows = xin.at[1 - c, pl.ds(k * 128, 128)]
        pltpu.make_async_remote_copy(
            src_ref=rows, dst_ref=rows, send_sem=in_send.at[k], recv_sem=in_recv.at[k],
            device_id=peer(dc=1), device_id_type=MESH).wait_recv()

    arrive(0, ph1)
    ph2[y] = part(ploc, c)[...] + ph1[...]
    for n, d in enumerate(TO):
        send(1 + n, ph2.at[y], ph2.at[y], dy=d)
    loads[5].wait()
    feed(0)
    service(0)
    for n, d in enumerate(TO):
        arrive(1 + n, ph2.at[wrap(y - d)])
    mine_sum = (ph2[0] + ph2[1]) + (ph2[2] + ph2[3])
    part(pk, c)[...] = mine_sum
    pgb[c, f] = mine_sum.astype(BF)
    send(4, part(pk, c), part(pk, c), dc=1)
    for n, d in enumerate(TO):
        send(5 + n, pgb.at[c, f], pgb.at[c, f], dx=d)
    feed(1)
    arrive(4, part(pk, 1 - c))
    whole = pk[...]
    other = swap(whole)
    dup = jnp.concatenate([jnp.where(low_lane, whole, other), jnp.where(low_lane, other, whole)], axis=0)
    hi = dup.astype(BF)
    lo = dup - hi.astype(F32)
    lane320 = lax.broadcasted_iota(jnp.int32, (ROWS, 128), 1) < 64
    p2cat[:, 0:128] = hi
    p2cat[:, 128:256] = jnp.where(lane320, lo, 0.0).astype(BF)
    service(1)
    split = jnp.where(lane320, hi.astype(F32), lo).astype(BF)
    contract = (((0,), (0,)), ((), ()))
    gram = lax.dot_general(dup, jnp.where(lane320, dup, 0.0), contract, precision=lax.Precision.HIGHEST,
                           preferred_element_type=F32)[0:64] * 0.125
    for h in range(2):
        rloc[h, :, 1280:1408] = gram
        rloc[h, :, 1408:1536] = jnp.zeros((64, 128), F32)
    for h in range(2):

        @pl.loop(0, 5)
        def _(t):
            src = pl.ds(pl.multiple_of(h * HALF + t * 256, 256), 256)
            v = lax.dot_general(split, dl[:, src], contract, preferred_element_type=F32)
            v = v + lax.dot_general(split, er[:, src], contract, preferred_element_type=F32)
            rloc[h, :, pl.ds(pl.multiple_of(t * 256, 256), 256)] = v[0:64] + v[64:128]

    send(8, rloc.at[1 - c], rin, dc=1)
    feed(2)
    service(2)
    for n, d in enumerate(TO):
        arrive(5 + n, pgb.at[c, shard(-d, 0)])
    row4 = pl.ds(z * 4, 4)
    for n, d in enumerate(TO):
        send(9 + n, pgb.at[c, row4], pgb.at[c, row4], dz=d)
    arrive(8, rin)
    racc[...] = rloc[c] + rin[...]

    def rows16(k):
        return pl.ds(pl.multiple_of(k * 16, 16), 16)

    for n, d in enumerate(TO):
        send(12 + n, racc.at[rows16(wrap(y + d))], yin.at[n], dy=d)
    service(3)
    feed(3)
    for n in range(3):
        arrive(12 + n, yin.at[n])
    s16[...] = (racc[rows16(y), :] + yin[0]) + (yin[1] + yin[2])

    def block(ref, k):
        return ref.at[pl.ds(pl.multiple_of((k // 2) * 8, 8), 8), pl.ds(pl.multiple_of(lax.rem(k, 2) * 768, 128), 768)]

    for n, d in enumerate(TO):
        send(15 + n, block(s16, wrap(x + d)), xrs.at[n], dx=d)
    service(4)
    for n in range(3):
        arrive(15 + n, xrs.at[n])
    zrs[z] = (block(s16, x)[...] + xrs[0]) + (xrs[1] + xrs[2])
    for n, d in enumerate(TO):
        send(18 + n, zrs.at[z], zrs.at[z], dz=d)
    service(5)
    for n, d in enumerate(TO):
        arrive(18 + n, zrs.at[wrap(z - d)])
    block(t16, x)[...] = (zrs[0] + zrs[1]) + (zrs[2] + zrs[3])
    for n, d in enumerate(TO):
        send(21 + n, block(t16, x), block(t16, x), dx=d)
    for n, d in enumerate(TO):
        arrive(9 + n, pgb.at[c, pl.ds(wrap(z - d) * 4, 4)])
    send(24, pgb.at[c], pgb.at[c], dc=1)
    service(6)
    for n, d in enumerate(TO):
        arrive(21 + n, block(t16, wrap(x - d)))
    rfull[rows16(y), :] = t16[...]
    for n, d in enumerate(TO):
        send(25 + n, rfull.at[rows16(y)], rfull.at[rows16(y)], dy=d)

    def product(row, depth, first=False):
        ks = pl.ds(pl.multiple_of(row, 128), depth)

        for m in range(2):

            @pl.loop(0, 5)
            def _(n):
                ns = pl.ds(pl.multiple_of(n * 256, 256), 256)
                v = jnp.dot(xin[m, :, ks], wbuf[ks, ns], preferred_element_type=F32)
                if first:
                    acc[m, :, ns] = v
                else:
                    acc[m, :, ns] += v

    service(7)
    for k in range(4):
        fed(k)
    crossed(0, 0, 1, 2)
    crossed(1, 3, 4, 5)
    product(z * 1280, 1280, first=True)
    service(8)

    arrive(24, pgb.at[1 - c])

    @pl.loop(0, 16)
    def _(t):
        for h in range(2):
            v = pgb[h, t]
            pfull[pl.ds(pl.multiple_of(t * ROWS + h * 80, 16), 80), :] = v
            pfull[pl.ds(pl.multiple_of(t * ROWS + 160 + h * 80, 16), 80), :] = swap(v.astype(F32)).astype(BF)

    for m in range(2):
        for k in range(4):
            v = jnp.dot(xin[m, :, k * 1280 : (k + 1) * 1280], pfull[k * 1280 : (k + 1) * 1280, :],
                        preferred_element_type=F32)
            if k == 0:
                tacc[m] = v
            else:
                tacc[m] += v
    lane512 = lax.broadcasted_iota(jnp.int32, (512, 128), 1) < 64
    for m in range(2):
        v = tacc[m] * -1.33
        v = jnp.where(lane512, v, swap(v))
        hi = v.astype(BF)
        tcat[m, :, 0:128] = hi
        tcat[m, :, 128:256] = jnp.where(lane512, v - hi.astype(F32), 0.0).astype(BF)
    service(9)

    for n, d in enumerate(TO):
        arrive(25 + n, rfull.at[rows16(wrap(y - d))])
    lane64 = lax.broadcasted_iota(jnp.int32, (64, 128), 1)
    sub64 = lax.broadcasted_iota(jnp.int32, (64, 128), 0)
    a = jnp.where(lane64 == sub64 + 64, 1.0, jnp.where(lane64 < 64, rfull[:, 1280:1408], 0.0))
    for k in range(64):
        row = a[k : k + 1, :] / a[k : k + 1, k : k + 1]
        a = jnp.where(sub64 == k, row, a - a[:, k : k + 1] * row)
    inverse = swap(a)[:, 0:64]
    wf[c] = jnp.dot(inverse, rfull[:, 0:1280], precision=lax.Precision.HIGHEST, preferred_element_type=F32) * 0.125
    send(28, wf.at[c], wf.at[c], dc=1)
    service(10)
    arrive(28, wf.at[1 - c])
    for h in range(2):
        v = wf[h]
        hi = v.astype(BF)
        wcat[h, 0:64, :] = hi
        wcat[h, 64:128, :] = (v - hi.astype(F32)).astype(BF)
        wcat[h, 128:192, :] = hi
        wcat[h, 192:256, :] = jnp.zeros((64, HALF), BF)

    loads[6].wait()
    loads[7].wait()
    for h in range(2):

        @pl.loop(0, ROWS // 32)
        def _(t):
            r = pl.ds(pl.multiple_of(t * 32, 32), 32)
            cols = slice(h * HALF, (h + 1) * HALF)
            approx = jnp.dot(p2cat[r, :], wcat[h], preferred_element_type=F32)
            merged = dl[r, cols].astype(F32) + er[r, cols].astype(F32)
            dl[r, cols] = (merged - approx).astype(BF)
            m = 0.9 * mom[h, r, :] + approx
            mom[h, r, :] = m
            prm[h, r, :] = prm[h, r, :] - 0.7 * (approx + 0.9 * m)

    stores = []

    def start_store(src, dst):
        copy = pltpu.make_async_copy(src, dst, store.at[len(stores)])
        copy.start()
        stores.append(copy)

    start_store(dl, new_error.at[0])
    for h in range(2):
        start_store(prm.at[h], new_params.at[:, pl.ds(h * HALF, HALF)])
        start_store(mom.at[h], new_momentum.at[:, pl.ds(h * HALF, HALF)])

    service(11)
    crossed(0, 3, 5, 7, 9)
    crossed(1, 0, 6, 7, 8)
    product(wrap(z - 1) * 1280, 1280)
    service(12)
    crossed(0, 4, 6, 8, 10)
    crossed(1, 1, 9, 10, 11)
    product(wrap(z + 1) * 1280, 1280)
    service(13)
    for m in range(2):

        @pl.loop(0, 5)
        def _(n):
            ns = pl.ds(pl.multiple_of(n * 256, 256), 256)
            acc[m, :, ns] += jnp.dot(tcat[m], wcat[c, :, ns], preferred_element_type=F32)

    crossed(0, 11, 12, 13)
    crossed(1, 2, 12, 13)
    last = wrap(z + 2) * 1280
    pair = x // 2
    service(14)
    product(last + pair * 640, 640)
    crossed(0, 14)
    crossed(1, 14)
    ks = pl.ds(pl.multiple_of(last + (1 - pair) * 640, 128), 640)

    def final(m, n):
        ns = pl.ds(n * 256, 256)
        return (acc[m, :, ns] + jnp.dot(xin[m, :, ks], wbuf[ks, ns], preferred_element_type=F32)).astype(BF)

    outs = []
    for n in range(5):
        sbuf[:, n * 256 : (n + 1) * 256] = final(1 - c, n)
        copy = pltpu.make_async_remote_copy(
            src_ref=sbuf.at[:, pl.ds(n * 256, 256)], dst_ref=obuf.at[c, :, pl.ds(n * 256, 256)],
            send_sem=out_send.at[n], recv_sem=out_recv.at[n], device_id=peer(dc=1), device_id_type=MESH)
        copy.start()
        outs.append(copy)
    for n in range(5):
        obuf[c, :, n * 256 : (n + 1) * 256] = final(c, n)
    start_store(obuf.at[c], outputs.at[:, mine(c * HALF)])
    for n in range(5):
        there = obuf.at[1 - c, :, pl.ds(n * 256, 256)]
        pltpu.make_async_remote_copy(
            src_ref=there, dst_ref=there, send_sem=out_send.at[n], recv_sem=out_recv.at[n],
            device_id=peer(dc=1), device_id_type=MESH).wait_recv()
    start_store(obuf.at[1 - c], outputs.at[:, mine((1 - c) * HALF)])

    for copy in sent + in_copies + outs:
        copy.wait_send()
    for r in range(ROUNDS):
        for k in range(4):
            plane_copy(r, k).wait_send()
    for way in range(2):
        for j in range(15):
            cross_copy(way, j).wait_send()
    for copy in stores:
        copy.wait()


def body(delta, error, params, momentum, q_init, inputs):
    dma = pltpu.SemaphoreType.DMA
    v = pltpu.VMEM
    anywhere = pl.BlockSpec(memory_space=pl.ANY)
    return tuple(pl.pallas_call(
        kernel,
        name="outer_step",
        out_shape=[
            jax.ShapeDtypeStruct((ROWS, 2560), F32),
            jax.ShapeDtypeStruct((ROWS, 2560), F32),
            jax.ShapeDtypeStruct((1, ROWS, 2560), BF),
            jax.ShapeDtypeStruct((512, 2560), BF),
        ],
        in_specs=[anywhere] * 6,
        out_specs=[anywhere] * 4,
        scratch_shapes=[
            v((5120, HALF), BF), v((2, 512, 5120), BF), v((2, 512, HALF), F32),
            v((ROWS, 2560), BF), v((ROWS, 2560), BF), v((2, ROWS, HALF), F32), v((2, ROWS, HALF), F32),
            v((64, 2560), F32), v((128, 2560), BF), v((2, 512, HALF), BF), v((512, HALF), BF),
            v((160, 128), F32), v((80, 128), F32), v((4, 80, 128), F32), v((160, 128), F32), v((ROWS, 256), BF),
            v((2, 16, 80, 128), BF), v((5120, 128), BF), v((2, 512, 128), F32), v((2, 512, 256), BF),
            v((2, 64, WIDE), F32), v((64, WIDE), F32), v((64, WIDE), F32), v((3, 16, WIDE), F32), v((16, WIDE), F32), v((16, WIDE), F32),
            v((3, 8, 768), F32), v((4, 8, 768), F32), v((64, WIDE), F32), v((2, 64, HALF), F32), v((2, 256, HALF), BF),
            dma((ROUNDS, 4)), dma((ROUNDS, 4)), dma((2, 15)), dma((2, 15)), dma((8,)), dma((8,)),
            dma((29,)), dma((29,)), dma((4,)), dma((4,)), dma((5,)), dma((5,)),
        ],
        compiler_params=pltpu.CompilerParams(collective_id=0, has_side_effects=True, vmem_limit_bytes=60 * 2**20),
        cost_estimate=pl.CostEstimate(flops=15 * 10**9, bytes_accessed=30 * 10**6, transcendentals=0),
    )(delta, error, params, momentum, q_init.T, inputs))


def solution(mesh):
    in_specs = (
        P("island", "fsdp", None),
        P("island", "fsdp", None),
        P("fsdp", None),
        P("fsdp", None),
        P(),
        P(("island", "fsdp"), None),
    )
    out_specs = (
        P("fsdp", None),
        P("fsdp", None),
        P("island", "fsdp", None),
        P(("island", "fsdp"), None),
    )
    return jax.shard_map(body, mesh=mesh, in_specs=in_specs, out_specs=out_specs, check_vma=False)
```

time: 517 us -> 108 us (0.21)
  waiting for transfers between devices: 375 us -> 0 us
  Pallas kernels: 0 us -> 96.4 us
  blocking collectives: 60.3 us -> 0 us
  matrix products: 49.9 us -> 0 us
  between operations: 13.8 us -> 0.65 us
  other arithmetic: 12.1 us -> 0 us
    psum x2 -> x0, waiting for transfers between devices: 216 us -> none  [the longest x1 158 us: body(): q_sum = lax.psum(q_part, ('island', 'fsdp'))]
    all_gather x1 -> x0, waiting for transfers between devices: 158 us -> none  [body(): lax.all_gather(weights, 'fsdp', axis=0, tiled=True)]
    pallas_call x0 -> x1, Pallas kernels: none -> 96.4 us  [body(): pl.pallas_call(kernel, name='outer_step', out_shape=[jax.ShapeDtypeStruct...]
    psum x1 -> x0, blocking collectives: 60.3 us -> none  [body(): gram = lax.psum(jnp.dot(p_sum.T, p_sum, precision=highest), 'fsdp')]
    dot_general x5 -> x0, matrix products: 48.7 us -> none  [the longest x1 21.6 us: body(): jnp.dot(inputs, lax.all_gather(weights, 'fsdp', axis=0, tiled=True), pref...]
    another operation x5 -> x0, other arithmetic: 12.1 us -> none  [the longest x3 6.52 us: body(): lower = jnp.linalg.cholesky(gram)]
    unnamed x5 -> x10, local copies, waits for them, and re-layouts: 5.41 us -> 10.4 us
  transfers between devices with their start and end apart: 3 -> 0, of which waited for: 3 -> 0; matrix products, arithmetic and copies ran while one was open for 0% -> 0% of each run, Pallas kernels for 0% -> 0%
where the time goes in v2:
time: 108 us
  Pallas kernels  96.4 us (89%)
  local copies, waits for them, and re-layouts  10.4 us (10%)
    pallas_call x1, Pallas kernels, body(): pl.pallas_call(kernel, name='outer_step', out_shape=[jax.ShapeDtypeStruct...  96.4 us
    unnamed x10, local copies, waits for them, and re-layouts  10.4 us

profile of v2, /device:TPU:1, one launch (start us, length us, event | category | flops | bytes accessed | tf_op | source)
XLA Modules:
  0.0 107.5 jit_solution(97220932623676900)
XLA Ops:
  0.6 96.4 %outer_step.1 = (f32[320,2560]{1,0:T(8,128)}, f32[320,2560]{1,0:T(8,128)}, bf16[1,320,2560]{2,1,0:T(8,128)(2,1)}, bf16[512,2560]{1,0:T(8,128)(2,1)}) custom-call(bf16[1,320,2560]{2,1,0:T(8,128)(2,1)} %delta.1, bf16[1,320,2560]{2,1,0:T(8,128)(2,1)} %error.1, f32[320,2560]{1,0:T(8,128)} %params.1, f32[320,2560]{1,0:T(8,128)} %momentum.1, f32[64,2560]{1,0:T(8,128)} %bitcast.1, ...), custom_call_target="tpu_custom_call" | custom-call | flops 15000000512 | bytes 30000000 | tf_op jit(solution)/shard_map/outer_step/pallas_call | solution.py:458
  97.0 0.0 copy-start
  97.1 4.0 %copy.14 = f32[320,2560]{1,0:T(8,128)} copy(f32[320,2560]{1,0:T(8,128)} %get-tuple-element.8) | data formatting | bytes 6553600
  101.1 0.0 copy-done
  101.1 0.0 copy-start.2
  101.1 1.7 %copy.15 = f32[320,2560]{1,0:T(8,128)} copy(f32[320,2560]{1,0:T(8,128)S(1)} %copy-done) | data formatting | bytes 6553600
  102.8 0.9 copy-done.2
  103.7 0.0 copy-start.1
  103.7 1.2 %copy.16 = bf16[1,320,2560]{2,1,0:T(8,128)(2,1)} copy(bf16[1,320,2560]{2,1,0:T(8,128)(2,1)S(1)} %copy-done.2) | data formatting | bytes 3276800
  104.8 1.2 %copy-done.1 = bf16[512,2560]{1,0:T(8,128)(2,1)S(1)} copy-done((bf16[512,2560]{1,0:T(8,128)(2,1)S(1)}, bf16[512,2560]{1,0:T(8,128)(2,1)}, u32[]{:S(2)}) %copy-start.1) | copy-done | bytes 2621464
  106.0 1.5 %copy.17 = bf16[512,2560]{1,0:T(8,128)(2,1)} copy(bf16[512,2560]{1,0:T(8,128)(2,1)S(1)} %copy-done.1) | data formatting | bytes 5242880
Async XLA Ops:
  97.0 4.0 %copy-start = (f32[320,2560]{1,0:T(8,128)S(1)}, f32[320,2560]{1,0:T(8,128)}, u32[]{:S(2)}) copy-start(f32[320,2560]{1,0:T(8,128)} %get-tuple-element.9) | copy-start | bytes 9830404
  101.1 2.6 %copy-start.2 = (bf16[1,320,2560]{2,1,0:T(8,128)(2,1)S(1)}, bf16[1,320,2560]{2,1,0:T(8,128)(2,1)}, u32[]{:S(2)}) copy-start(bf16[1,320,2560]{2,1,0:T(8,128)(2,1)} %get-tuple-element.10) | copy-start | bytes 4915204
  103.7 2.3 %copy-start.1 = (bf16[512,2560]{1,0:T(8,128)(2,1)S(1)}, bf16[512,2560]{1,0:T(8,128)(2,1)}, u32[]{:S(2)}) copy-start(bf16[512,2560]{1,0:T(8,128)(2,1)} %get-tuple-element.11) | copy-start | bytes 7864324

commit v3 on v2

v3 whole, which is shorter than its diff:
```python
import jax
import jax.numpy as jnp
from jax import lax
from jax.experimental import pallas as pl
from jax.experimental.pallas import tpu as pltpu
from jax.sharding import PartitionSpec as P

BF = jnp.bfloat16
F32 = jnp.float32
MESH = pl.DeviceIdType.MESH

ROWS = 320
HALF = 1280
UNIT = 640
STREAM = 112
CROSS = 48
ROUNDS = 15
LINES = 64
VMEM_MIB = 60
OFFS = (0, -1, 1, 2)


def plan():
    table = [[None] * 4 for _ in range(ROUNDS)]
    for side, (h0, h1, back) in enumerate(((0, 1, -1), (1, 0, 1))):
        x, z = side, 2 + side
        table[0][x], table[1][x], table[2][x] = ("a", 0, 0, h0), ("a", 0, 0, h1), ("a", back, 0, h0)
        table[0][z], table[1][z], table[2][z] = ("b", 0, 0, h0), ("b", 0, 0, h1), ("b", 0, back, h0)
        for k, off in enumerate(OFFS):
            table[3 + 3 * k][x] = ("b", 0, off, h0)
            table[4 + 3 * k][x] = ("b", 0, off, h1)
            table[5 + 3 * k][x] = ("b", back, off, h0)
            table[3 + 2 * k][z] = ("a", off, 0, h0)
            table[4 + 2 * k][z] = ("a", off, 0, h1)
            table[11 + k][z] = ("a", off, back, h0)
    return table


TABLE = plan()
UP = [(1, -1, 0), (1, 1, 0), (2, 2, 0)]
for _k, _o in enumerate(OFFS):
    UP += [(4 + 2 * _k, _o, -1), (4 + 2 * _k, _o, 1)]
UP += [(11 + _k, _o, 2) for _k, _o in enumerate(OFFS)]
DOWN = [(1, 0, -1), (1, 0, 1), (2, 0, 2)]
for _k, _o in enumerate(OFFS):
    DOWN += [(4 + 3 * _k, -1, _o), (4 + 3 * _k, 1, _o), (5 + 3 * _k, 2, _o)]


def kernel(
    delta, error, params, momentum, q_init, inputs,
    left_out, right_out, outputs,
    wbuf, xin, acc, dl, er, prm, mom, q32, q2, obuf, sbuf,
    ploc, ph1, ph2, pk, p2cat, pgb, pfull, tcat,
    gx, gz, inverse, split, rloc, rin, racc, yin, s16, t16, xrs, zrs, rfull, wf, wcat,
    plane_send, plane_recv, cross_send, cross_recv, load, store,
    c_send, c_recv, in_send, in_recv, out_send, out_recv,
):
    i, f = lax.axis_index("island"), lax.axis_index("fsdp")
    y, c = i // 2, lax.rem(i, 2)
    z, x = f // 4, lax.rem(f, 4)
    parity = lax.rem(y, 2)
    u, v = x + c * (z - x), z + c * (x - z)

    def wrap(v):
        return lax.rem(v + 4, 4)

    def peer(dx=0, dy=0, dz=0, dc=0):
        return (wrap(y + dy) * 2 + lax.rem(c + dc, 2), wrap(z + dz) * 4 + wrap(x + dx))

    def along_u(d):
        return dict(dx=d * (1 - c), dz=d * c)

    def along_v(d):
        return dict(dx=d * c, dz=d * (1 - c))

    def shard(dx, dz):
        return wrap(z + dz) * 4 + wrap(x + dx)

    PEERS = [dict(dx=1), dict(dx=-1), dict(dx=2), dict(dy=1), dict(dy=-1), dict(dy=2),
             dict(dz=1), dict(dz=-1), dict(dz=2), dict(dc=1)]
    LINKS = [dict(dx=1), dict(dx=-1), dict(dz=1), dict(dz=-1)]

    barrier = pltpu.get_barrier_semaphore()
    for p in PEERS:
        pl.semaphore_signal(barrier, inc=1, device_id=peer(**p), device_id_type=MESH)

    def mine(col):
        return pl.ds(pl.multiple_of(col, 128), HALF)

    loads = {}

    def start_load(n, src, dst):
        loads[n] = pltpu.make_async_copy(src, dst, load.at[n])
        loads[n].start()

    start_load(0, params.at[:, mine(c * HALF)], prm)
    start_load(1, momentum.at[:, mine(c * HALF)], mom)
    start_load(2, q_init, q32)
    start_load(3, delta.at[0], dl)
    start_load(4, error.at[0], er)

    loads[0].wait()
    loads[1].wait()

    @pl.loop(0, ROWS // 32)
    def _(t):
        r = pl.ds(pl.multiple_of(t * 32, 32), 32)
        b = prm[r, :] - 0.567 * mom[r, :]
        wbuf[pl.ds(pl.multiple_of(f * ROWS + t * 32, 32), 32), :] = b.astype(BF)

    def swap(v):
        return pltpu.roll(v, 64, 1)

    def low(rows):
        return lax.broadcasted_iota(jnp.int32, (rows, 128), 1) < 64

    loads[2].wait()
    q = q32[...]
    hi = q.astype(BF)
    q2[0:64, :] = hi
    q2[64:128, :] = (q - hi.astype(F32)).astype(BF)
    loads[3].wait()
    loads[4].wait()
    last_dims = (((1,), (1,)), ((), ()))
    p_loc = lax.dot_general(dl[...], q2[...], last_dims, preferred_element_type=F32)
    p_loc = p_loc + lax.dot_general(er[...], q2[...], last_dims, preferred_element_type=F32)
    p_loc = p_loc + swap(p_loc)
    ploc[...] = jnp.where(low(160), p_loc[0:160], p_loc[160:320])

    pl.semaphore_wait(barrier, len(PEERS))

    sent = []

    def send(n, src, dst, **to):
        copy = pltpu.make_async_remote_copy(
            src_ref=src, dst_ref=dst, send_sem=c_send.at[n], recv_sem=c_recv.at[n],
            device_id=peer(**to), device_id_type=MESH)
        copy.start()
        sent.append(copy)

    def arrive(n, dst):
        pltpu.make_async_remote_copy(
            src_ref=dst, dst_ref=dst, send_sem=c_send.at[n], recv_sem=c_recv.at[n],
            device_id=peer(dc=1), device_id_type=MESH).wait_recv()

    TO = (1, -1, 2)

    def region(stream, dx, dz, h):
        row = shard(dx, dz) * ROWS + CROSS * parity + (0 if stream == "a" else 160)
        return wbuf.at[pl.ds(pl.multiple_of(row, 16), STREAM), pl.ds(h * UNIT, UNIT)]

    def plane_copy(r, k, arriving=False):
        stream, dx, dz, h = TABLE[r][k]
        if arriving:
            step = -1 if k % 2 == 0 else 1
            dx, dz = (dx + step, dz) if k < 2 else (dx, dz + step)
        here = region(stream, dx, dz, h)
        return pltpu.make_async_remote_copy(
            src_ref=here, dst_ref=here, send_sem=plane_send.at[r, k], recv_sem=plane_recv.at[r, k],
            device_id=peer(**LINKS[k]), device_id_type=MESH)

    def cross_copy(way, j, arriving=False):
        _, dx, dz = (UP, DOWN)[way][j]
        par = 1 - parity if arriving else parity
        row = shard(dx, dz) * ROWS + 160 * way + STREAM * par
        here = wbuf.at[pl.ds(pl.multiple_of(row, 16), CROSS), :]
        return pltpu.make_async_remote_copy(
            src_ref=here, dst_ref=here, send_sem=cross_send.at[way, j], recv_sem=cross_recv.at[way, j],
            device_id=peer(dy=1 if way == 0 else -1), device_id_type=MESH)

    def issue(r):
        for k in range(4):
            plane_copy(r, k).start()

    def cross(*js):
        for j in js:
            for way in range(2):
                cross_copy(way, j).start()

    def got(q):
        for k in range(4):
            plane_copy(q, k, arriving=True).wait_recv()

    def go(q, hold=False):
        if q + 2 < ROUNDS:
            issue(q + 2)
        if not hold:
            for way in range(2):
                for j, (need, _, _) in enumerate((UP, DOWN)[way]):
                    if need == q:
                        cross_copy(way, j).start()

    def crossed(way, *js):
        for j in js:
            cross_copy(way, j, arriving=True).wait_recv()

    def part(ref, k):
        return ref.at[pl.ds(pl.multiple_of(k * 80, 16), 80)]

    send(0, part(ploc, 1 - c), ph1, dc=1)
    issue(0)
    issue(1)
    start_load(5, inputs, xin.at[c])
    arrive(0, ph1)
    ph2[y] = part(ploc, c)[...] + ph1[...]
    for n, d in enumerate(TO):
        send(1 + n, ph2.at[y], ph2.at[y], dy=d)

    in_copies = []

    def feed(k):
        rows = xin.at[c, pl.ds(k * 128, 128)]
        copy = pltpu.make_async_remote_copy(
            src_ref=rows, dst_ref=rows, send_sem=in_send.at[k], recv_sem=in_recv.at[k],
            device_id=peer(dc=1), device_id_type=MESH)
        copy.start()
        in_copies.append(copy)

    def fed(k):
        rows = xin.at[1 - c, pl.ds(k * 128, 128)]
        pltpu.make_async_remote_copy(
            src_ref=rows, dst_ref=rows, send_sem=in_send.at[k], recv_sem=in_recv.at[k],
            device_id=peer(dc=1), device_id_type=MESH).wait_recv()

    loads[5].wait()
    feed(0)
    got(0)
    go(0)

    for n, d in enumerate(TO):
        arrive(1 + n, ph2.at[wrap(y - d)])
    mine_sum = (ph2[0] + ph2[1]) + (ph2[2] + ph2[3])
    part(pk, c)[...] = mine_sum
    own = v * 4 + u
    pgb[c, own] = mine_sum.astype(BF)
    send(4, part(pk, c), part(pk, c), dc=1)
    for n, d in enumerate(TO):
        send(5 + n, pgb.at[c, own], pgb.at[c, own], **along_u(d))
    arrive(4, part(pk, 1 - c))
    whole = pk[...]
    other = swap(whole)
    dup = jnp.concatenate([jnp.where(low(160), whole, other), jnp.where(low(160), other, whole)], axis=0)
    low320 = low(ROWS)
    hi = dup.astype(BF)
    lo = dup - hi.astype(F32)
    p2cat[:, 0:128] = hi
    p2cat[:, 128:256] = jnp.where(low320, lo, 0.0).astype(BF)
    gram = lax.dot_general(dup, dup, (((0,), (0,)), ((), ())), precision=lax.Precision.HIGHEST,
                           preferred_element_type=F32)
    gx[u] = jnp.where(low(32), gram[0:32], gram[32:64])
    for n, d in enumerate(TO):
        send(29 + n, gx.at[u], gx.at[u], **along_u(d))
    got(1)
    go(1, hold=True)
    cross(0)
    split[...] = jnp.where(low320, hi.astype(F32), lo).T.astype(BF)
    for h in range(2):
        for t in range(2):
            src = slice(h * HALF + t * 640, h * HALF + (t + 1) * 640)
            raw = jnp.dot(split[...], dl[:, src], preferred_element_type=F32)
            raw = raw + jnp.dot(split[...], er[:, src], preferred_element_type=F32)
            rloc[h, :, t * 640 : (t + 1) * 640] = raw[0:64] + raw[64:128]

    send(8, rloc.at[1 - c], rin, dc=1)
    feed(1)
    got(2)
    for n, d in enumerate(TO):
        arrive(29 + n, gx.at[wrap(u - d)])
    gz[v] = (gx[0] + gx[1]) + (gx[2] + gx[3])
    for n, d in enumerate(TO):
        send(32 + n, gz.at[v], gz.at[v], **along_v(d))
    for n, d in enumerate(TO):
        arrive(5 + n, pgb.at[c, v * 4 + wrap(u - d)])
    row4 = pl.ds(v * 4, 4)
    for n, d in enumerate(TO):
        send(9 + n, pgb.at[c, row4], pgb.at[c, row4], **along_v(d))
    go(2, hold=True)
    arrive(8, rin)
    racc[...] = rloc[c] + rin[...]

    def rows16(k):
        return pl.ds(pl.multiple_of(k * 16, 16), 16)

    for n, d in enumerate(TO):
        send(12 + n, racc.at[rows16(wrap(y + d))], yin.at[n], dy=d)
    cross(1, 2)
    feed(2)
    feed(3)
    got(3)
    for n, d in enumerate(TO):
        arrive(32 + n, gz.at[wrap(v - d)])
    gram = (gz[0] + gz[1]) + (gz[2] + gz[3])
    go(3)

    lane64 = lax.broadcasted_iota(jnp.int32, (64, 128), 1)
    sub64 = lax.broadcasted_iota(jnp.int32, (64, 128), 0)
    a = jnp.concatenate([gram, swap(gram)], axis=0)
    a = jnp.where(lane64 < 64, a, jnp.where(lane64 == sub64 + 64, 1.0, 0.0))

    def eliminate(a, first, end):
        for k in range(first, end):
            row = a[k : k + 1, :] / a[k : k + 1, k : k + 1]
            a = jnp.where(sub64 == k, row, a - a[:, k : k + 1] * row)
        return a

    a = eliminate(a, 0, 32)
    got(4)
    for n, d in enumerate(TO):
        arrive(9 + n, pgb.at[c, pl.ds(wrap(v - d) * 4, 4)])
    send(24, pgb.at[c], pgb.at[c], dc=1)
    go(4)
    a = eliminate(a, 32, 64)
    inverse[...] = swap(a)
    got(5)
    for n in range(3):
        arrive(12 + n, yin.at[n])
    s16[...] = (racc[rows16(y), :] + yin[0]) + (yin[1] + yin[2])

    def block(ref, k):
        return ref.at[pl.ds(pl.multiple_of((k // 2) * 8, 8), 8), pl.ds(pl.multiple_of(lax.rem(k, 2) * 640, 128), 640)]

    for n, d in enumerate(TO):
        send(15 + n, block(s16, wrap(u + d)), xrs.at[n], **along_u(d))
    go(5)

    arrive(24, pgb.at[1 - c])

    @pl.loop(0, 16)
    def _(t):
        for h in range(2):
            two = pgb[h, t]
            at = (t if h == 0 else lax.rem(t, 4) * 4 + t // 4) * ROWS + h * 80
            pfull[pl.ds(pl.multiple_of(at, 16), 80), :] = two
            pfull[pl.ds(pl.multiple_of(at + 160, 16), 80), :] = swap(two.astype(F32)).astype(BF)

    low512 = low(512)

    def left(m):
        part_m = jnp.dot(xin[m], pfull[...], preferred_element_type=F32) * -1.33
        part_m = jnp.where(low512, part_m, swap(part_m))
        hi = part_m.astype(BF)
        tcat[m, :, 0:128] = hi
        tcat[m, :, 128:256] = jnp.where(low512, part_m - hi.astype(F32), 0.0).astype(BF)

    def product(row, depth, m, first=False):
        ks = pl.ds(pl.multiple_of(row, 128), depth)
        term = jnp.dot(xin[m, :, ks], wbuf[ks, :], preferred_element_type=F32)
        if first:
            acc[m] = term
        else:
            acc[m] += term

    for k in range(4):
        fed(k)
    got(6)
    for n in range(3):
        arrive(15 + n, xrs.at[n])
    zrs[v] = (block(s16, u)[...] + xrs[0]) + (xrs[1] + xrs[2])
    for n, d in enumerate(TO):
        send(18 + n, zrs.at[v], zrs.at[v], **along_v(d))
    go(6)
    left(0)
    got(7)
    for n, d in enumerate(TO):
        arrive(18 + n, zrs.at[wrap(v - d)])
    block(t16, u)[...] = (zrs[0] + zrs[1]) + (zrs[2] + zrs[3])
    for n, d in enumerate(TO):
        send(21 + n, block(t16, u), block(t16, u), **along_u(d))
    go(7)
    left(1)
    got(8)
    for n, d in enumerate(TO):
        arrive(21 + n, block(t16, wrap(u - d)))
    rfull[rows16(y), :] = t16[...]
    for n, d in enumerate(TO):
        send(25 + n, rfull.at[rows16(y)], rfull.at[rows16(y)], dy=d)
    go(8)
    crossed(0, 0, 1, 2)
    crossed(1, 3, 4, 5)
    product(z * 1280, 1280, 0, first=True)
    got(9)
    go(9)
    product(z * 1280, 1280, 1, first=True)
    got(10)
    go(10)
    for n, d in enumerate(TO):
        arrive(25 + n, rfull.at[rows16(wrap(y - d))])

    wf[c] = jnp.dot(inverse[:, 0:64], rfull[...], precision=lax.Precision.HIGHEST, preferred_element_type=F32) * 0.125
    send(28, wf.at[c], wf.at[c], dc=1)
    got(11)
    go(11)
    crossed(0, 3, 5, 7, 9)
    crossed(1, 0, 6, 7, 8)
    product(wrap(z - 1) * 1280, 1280, 0)
    got(12)
    go(12)
    product(wrap(z - 1) * 1280, 1280, 1)
    arrive(28, wf.at[1 - c])
    for h in range(2):
        w = wf[h]
        hi = w.astype(BF)
        wcat[h, 0:64, :] = hi
        wcat[h, 64:128, :] = (w - hi.astype(F32)).astype(BF)
        wcat[h, 128:192, :] = hi
        wcat[h, 192:256, :] = jnp.zeros((64, HALF), BF)
    stores = []

    def start_store(src, dst):
        copy = pltpu.make_async_copy(src, dst, store.at[len(stores)])
        copy.start()
        stores.append(copy)

    start_store(p2cat, left_out)
    start_store(wcat, right_out)
    got(13)
    go(13)
    crossed(0, 4, 6, 8, 10)
    crossed(1, 1, 9, 10, 11)
    product(wrap(z + 1) * 1280, 1280, 0)
    got(14)
    go(14)
    product(wrap(z + 1) * 1280, 1280, 1)

    @pl.loop(0, 2)
    def _(m):
        acc[m] += jnp.dot(tcat[m], wcat[c], preferred_element_type=F32)

    crossed(0, 11, 12, 13)
    crossed(1, 2, 12, 13)
    last = wrap(z + 2) * 1280
    pair = x // 2
    for m in range(2):
        product(last + pair * 640, 640, m)
    crossed(0, 14)
    crossed(1, 14)
    ks = pl.ds(pl.multiple_of(last + (1 - pair) * 640, 128), 640)

    def final(m, t):
        rows = slice(t * 256, (t + 1) * 256)
        return (acc[m, rows, :] + jnp.dot(xin[m, rows, ks], wbuf[ks, :], preferred_element_type=F32)).astype(BF)

    outs = []
    for t in range(2):
        rows = pl.ds(t * 256, 256)
        sbuf[t * 256 : (t + 1) * 256, :] = final(1 - c, t)
        copy = pltpu.make_async_remote_copy(
            src_ref=sbuf.at[rows], dst_ref=obuf.at[c, rows],
            send_sem=out_send.at[t], recv_sem=out_recv.at[t], device_id=peer(dc=1), device_id_type=MESH)
        copy.start()
        outs.append(copy)
    for t in range(2):
        obuf[c, t * 256 : (t + 1) * 256, :] = final(c, t)
    start_store(obuf.at[c], outputs.at[:, mine(c * HALF)])
    for t in range(2):
        there = obuf.at[1 - c, pl.ds(t * 256, 256)]
        pltpu.make_async_remote_copy(
            src_ref=there, dst_ref=there, send_sem=out_send.at[t], recv_sem=out_recv.at[t],
            device_id=peer(dc=1), device_id_type=MESH).wait_recv()
    start_store(obuf.at[1 - c], outputs.at[:, mine((1 - c) * HALF)])

    for copy in sent + in_copies + outs:
        copy.wait_send()
    for r in range(ROUNDS):
        for k in range(4):
            plane_copy(r, k).wait_send()
    for way in range(2):
        for j in range(15):
            cross_copy(way, j).wait_send()
    for copy in stores:
        copy.wait()


def finish(delta, error, params, momentum, left, right, ready, new_params, new_momentum, new_error, outputs):
    outputs[...] = ready[...]
    for h in range(2):
        cols = slice(h * HALF, (h + 1) * HALF)
        approx = jnp.dot(left[...], right[h], preferred_element_type=F32)
        merged = delta[0, :, cols].astype(F32) + error[0, :, cols].astype(F32)
        new_error[0, :, cols] = (merged - approx).astype(BF)
        m = 0.9 * momentum[:, cols] + approx
        new_momentum[:, cols] = m
        new_params[:, cols] = params[:, cols] - 0.7 * (approx + 0.9 * m)


def body(delta, error, params, momentum, q_init, inputs):
    dma = pltpu.SemaphoreType.DMA
    v = pltpu.VMEM
    anywhere = pl.BlockSpec(memory_space=pl.ANY)
    left, right, ready = pl.pallas_call(
        kernel,
        name="outer_step",
        out_shape=[
            jax.ShapeDtypeStruct((ROWS, 256), BF),
            jax.ShapeDtypeStruct((2, 256, HALF), BF),
            jax.ShapeDtypeStruct((512, 2560), BF),
        ],
        in_specs=[anywhere] * 6,
        out_specs=[anywhere] * 3,
        scratch_shapes=[
            v((5120, HALF), BF), v((2, 512, 5120), BF), v((2, 512, HALF), F32),
            v((ROWS, 2560), BF), v((ROWS, 2560), BF), v((ROWS, HALF), F32), v((ROWS, HALF), F32),
            v((64, 2560), F32), v((128, 2560), BF), v((2, 512, HALF), BF), v((512, HALF), BF),
            v((160, 128), F32), v((80, 128), F32), v((4, 80, 128), F32), v((160, 128), F32), v((ROWS, 256), BF),
            v((2, 16, 80, 128), BF), v((5120, 128), BF), v((2, 512, 256), BF),
            v((4, 32, 128), F32), v((4, 32, 128), F32), v((64, 128), F32), v((128, ROWS), BF),
            v((2, 64, HALF), F32), v((64, HALF), F32), v((64, HALF), F32), v((3, 16, HALF), F32), v((16, HALF), F32), v((16, HALF), F32),
            v((3, 8, 640), F32), v((4, 8, 640), F32), v((64, HALF), F32), v((2, 64, HALF), F32), v((2, 256, HALF), BF),
            dma((ROUNDS, 4)), dma((ROUNDS, 4)), dma((2, 15)), dma((2, 15)), dma((8,)), dma((8,)),
            dma((35,)), dma((35,)), dma((4,)), dma((4,)), dma((2,)), dma((2,)),
        ],
        compiler_params=pltpu.CompilerParams(collective_id=0, has_side_effects=True, vmem_limit_bytes=VMEM_MIB * 2**20),
        cost_estimate=pl.CostEstimate(flops=15 * 10**9, bytes_accessed=30 * 10**6, transcendentals=0),
    )(delta, error, params, momentum, q_init.T, inputs)
    lines = pl.BlockSpec((LINES, 2560), lambda i: (i, 0))
    columns = pl.BlockSpec((512, 8 * LINES), lambda i: (0, i))
    boxed = pl.BlockSpec((1, LINES, 2560), lambda i: (0, i, 0))
    return tuple(pl.pallas_call(
        finish,
        name="finish",
        grid=(ROWS // LINES,),
        out_shape=[
            jax.ShapeDtypeStruct((ROWS, 2560), F32),
            jax.ShapeDtypeStruct((ROWS, 2560), F32),
            jax.ShapeDtypeStruct((1, ROWS, 2560), BF),
            jax.ShapeDtypeStruct((512, 2560), BF),
        ],
        in_specs=[
            boxed, boxed, lines, lines, pl.BlockSpec((LINES, 256), lambda i: (i, 0)),
            pl.BlockSpec((2, 256, HALF), lambda i: (0, 0, 0)), columns,
        ],
        out_specs=[lines, lines, boxed, columns],
        compiler_params=pltpu.CompilerParams(vmem_limit_bytes=VMEM_MIB * 2**20),
        cost_estimate=pl.CostEstimate(flops=500 * 10**6, bytes_accessed=24 * 10**6, transcendentals=0),
    )(delta, error, params, momentum, left, right, ready))


def solution(mesh):
    in_specs = (
        P("island", "fsdp", None),
        P("island", "fsdp", None),
        P("fsdp", None),
        P("fsdp", None),
        P(),
        P(("island", "fsdp"), None),
    )
    out_specs = (
        P("fsdp", None),
        P("fsdp", None),
        P("island", "fsdp", None),
        P(("island", "fsdp"), None),
    )
    return jax.shard_map(body, mesh=mesh, in_specs=in_specs, out_specs=out_specs, check_vma=False)
```

time: 108 us -> 94 us (0.87)
  local copies, waits for them, and re-layouts: 10.4 us -> 0 us
  Pallas kernels: 96.4 us -> 93 us
    pallas_call x1, Pallas kernels: 96.4 us -> 81.4 us  [body(): pl.pallas_call(kernel, name='outer_step', out_shape=[jax.ShapeDtypeStruct...]
    pallas_call x0 -> x1, Pallas kernels: none -> 11.6 us  [body(): pl.pallas_call(finish, name='finish', grid=(ROWS // LINES,), out_shape=[j...]
    unnamed x10 -> x0, local copies, waits for them, and re-layouts: 10.4 us -> none
where the time goes in v3:
time: 94 us; the launch traced here: 93.8 us
  Pallas kernels  93 us (99%)
    pallas_call x1, Pallas kernels, body(): pl.pallas_call(kernel, name='outer_step', out_shape=[jax.ShapeDtypeStruct...  81.4 us
    pallas_call x1, Pallas kernels, body(): pl.pallas_call(finish, name='finish', grid=(ROWS // LINES,), out_shape=[j...  11.6 us

profile of v3, /device:TPU:1, one launch (start us, length us, event | category | flops | bytes accessed | tf_op | source)
XLA Modules:
  0.0 93.8 jit_solution(17159134149526369078)
XLA Ops:
  0.6 81.4 %outer_step.1 = (bf16[320,256]{1,0:T(8,128)(2,1)}, bf16[2,256,1280]{2,1,0:T(8,128)(2,1)}, bf16[512,2560]{1,0:T(8,128)(2,1)}) custom-call(bf16[1,320,2560]{2,1,0:T(8,128)(2,1)} %delta.3, bf16[1,320,2560]{2,1,0:T(8,128)(2,1)} %error.3, f32[320,2560]{1,0:T(8,128)} %params.3, f32[320,2560]{1,0:T(8,128)} %momentum.3, f32[64,2560]{1,0:T(8,128)} %bitcast.1, ...), custom_call_target="tpu_custom_call" | custom-call | flops 15000000512 | bytes 30000000 | tf_op jit(solution)/shard_map/outer_step/pallas_call | solution.py:490
  82.0 11.6 %finish.1 = (f32[320,2560]{1,0:T(8,128)}, f32[320,2560]{1,0:T(8,128)}, bf16[1,320,2560]{2,1,0:T(8,128)(2,1)}, bf16[512,2560]{1,0:T(8,128)(2,1)}) custom-call(bf16[1,320,2560]{2,1,0:T(8,128)(2,1)} %delta.3, bf16[1,320,2560]{2,1,0:T(8,128)(2,1)} %error.3, f32[320,2560]{1,0:T(8,128)} %params.3, f32[320,2560]{1,0:T(8,128)} %momentum.3, ...), custom_call_target="tpu_custom_call" | custom-call | flops 500000000 | bytes 24000000 | tf_op jit(solution)/shard_map/finish/pallas_call | solution.py:518

commit v4 on v3

--- a/solution.py
+++ b/solution.py
@@ -15,7 +15,7 @@
 STREAM = 112
 CROSS = 48
 ROUNDS = 15
-LINES = 64
+LINES = 160
 VMEM_MIB = 60
 OFFS = (0, -1, 1, 2)
 
@@ -390,12 +390,6 @@
     send(28, wf.at[c], wf.at[c], dc=1)
     got(11)
     go(11)
-    crossed(0, 3, 5, 7, 9)
-    crossed(1, 0, 6, 7, 8)
-    product(wrap(z - 1) * 1280, 1280, 0)
-    got(12)
-    go(12)
-    product(wrap(z - 1) * 1280, 1280, 1)
     arrive(28, wf.at[1 - c])
     for h in range(2):
         w = wf[h]
@@ -413,6 +407,17 @@
 
     start_store(p2cat, left_out)
     start_store(wcat, right_out)
+
+    @pl.loop(0, 2)
+    def _(m):
+        acc[m] += jnp.dot(tcat[m], wcat[c], preferred_element_type=F32)
+
+    got(12)
+    go(12)
+    crossed(0, 3, 5, 7, 9)
+    crossed(1, 0, 6, 7, 8)
+    product(wrap(z - 1) * 1280, 1280, 0)
+    product(wrap(z - 1) * 1280, 1280, 1)
     got(13)
     go(13)
     crossed(0, 4, 6, 8, 10)
@@ -421,10 +426,6 @@
     got(14)
     go(14)
     product(wrap(z + 1) * 1280, 1280, 1)
-
-    @pl.loop(0, 2)
-    def _(m):
-        acc[m] += jnp.dot(tcat[m], wcat[c], preferred_element_type=F32)
 
     crossed(0, 11, 12, 13)
     crossed(1, 2, 12, 13)

time: 94 us -> 90.7 us (0.965)
  Pallas kernels: 93 us -> 89.7 us
    pallas_call x1, Pallas kernels: 11.6 us -> 9.05 us  [body(): pl.pallas_call(finish, name='finish', grid=(ROWS // LINES,), out_shape=[j...]
where the time goes in v4:
time: 90.7 us; the launch traced here: 90.5 us
  Pallas kernels  89.7 us (99%)
    pallas_call x1, Pallas kernels, body(): pl.pallas_call(kernel, name='outer_step', out_shape=[jax.ShapeDtypeStruct...  80.7 us
    pallas_call x1, Pallas kernels, body(): pl.pallas_call(finish, name='finish', grid=(ROWS // LINES,), out_shape=[j...  9.05 us

profile of v4, /device:TPU:1, one launch (start us, length us, event | category | flops | bytes accessed | tf_op | source)
XLA Modules:
  0.0 90.5 jit_solution(17962064343671801921)
XLA Ops:
  0.6 80.7 %outer_step.1 = (bf16[320,256]{1,0:T(8,128)(2,1)}, bf16[2,256,1280]{2,1,0:T(8,128)(2,1)}, bf16[512,2560]{1,0:T(8,128)(2,1)}) custom-call(bf16[1,320,2560]{2,1,0:T(8,128)(2,1)} %delta.3, bf16[1,320,2560]{2,1,0:T(8,128)(2,1)} %error.3, f32[320,2560]{1,0:T(8,128)} %params.3, f32[320,2560]{1,0:T(8,128)} %momentum.3, f32[64,2560]{1,0:T(8,128)} %bitcast.1, ...), custom_call_target="tpu_custom_call" | custom-call | flops 15000000512 | bytes 30000000 | tf_op jit(solution)/shard_map/outer_step/pallas_call | solution.py:491
  81.3 9.0 %finish.1 = (f32[320,2560]{1,0:T(8,128)}, f32[320,2560]{1,0:T(8,128)}, bf16[1,320,2560]{2,1,0:T(8,128)(2,1)}, bf16[512,2560]{1,0:T(8,128)(2,1)}) custom-call(bf16[1,320,2560]{2,1,0:T(8,128)(2,1)} %delta.3, bf16[1,320,2560]{2,1,0:T(8,128)(2,1)} %error.3, f32[320,2560]{1,0:T(8,128)} %params.3, f32[320,2560]{1,0:T(8,128)} %momentum.3, ...), custom_call_target="tpu_custom_call" | custom-call | flops 500000000 | bytes 24000000 | tf_op jit(solution)/shard_map/finish/pallas_call | solution.py:519

commit v5 on v4

--- a/solution.py
+++ b/solution.py
@@ -15,7 +15,7 @@
 STREAM = 112
 CROSS = 48
 ROUNDS = 15
-LINES = 160
+WIDTH = 640
 VMEM_MIB = 60
 OFFS = (0, -1, 1, 2)
 
@@ -474,14 +474,12 @@
 
 def finish(delta, error, params, momentum, left, right, ready, new_params, new_momentum, new_error, outputs):
     outputs[...] = ready[...]
-    for h in range(2):
-        cols = slice(h * HALF, (h + 1) * HALF)
-        approx = jnp.dot(left[...], right[h], preferred_element_type=F32)
-        merged = delta[0, :, cols].astype(F32) + error[0, :, cols].astype(F32)
-        new_error[0, :, cols] = (merged - approx).astype(BF)
-        m = 0.9 * momentum[:, cols] + approx
-        new_momentum[:, cols] = m
-        new_params[:, cols] = params[:, cols] - 0.7 * (approx + 0.9 * m)
+    approx = jnp.dot(left[...], right[0], preferred_element_type=F32)
+    merged = delta[0].astype(F32) + error[0].astype(F32)
+    new_error[0] = (merged - approx).astype(BF)
+    m = 0.9 * momentum[...] + approx
+    new_momentum[...] = m
+    new_params[...] = params[...] - 0.7 * (approx + 0.9 * m)
 
 
 def body(delta, error, params, momentum, q_init, inputs):
@@ -513,13 +511,14 @@
         compiler_params=pltpu.CompilerParams(collective_id=0, has_side_effects=True, vmem_limit_bytes=VMEM_MIB * 2**20),
         cost_estimate=pl.CostEstimate(flops=15 * 10**9, bytes_accessed=30 * 10**6, transcendentals=0),
     )(delta, error, params, momentum, q_init.T, inputs)
-    lines = pl.BlockSpec((LINES, 2560), lambda i: (i, 0))
-    columns = pl.BlockSpec((512, 8 * LINES), lambda i: (0, i))
-    boxed = pl.BlockSpec((1, LINES, 2560), lambda i: (0, i, 0))
+    steps = HALF // WIDTH
+    lines = pl.BlockSpec((ROWS, WIDTH), lambda i: (0, i))
+    columns = pl.BlockSpec((512, WIDTH), lambda i: (0, i))
+    boxed = pl.BlockSpec((1, ROWS, WIDTH), lambda i: (0, 0, i))
     return tuple(pl.pallas_call(
         finish,
         name="finish",
-        grid=(ROWS // LINES,),
+        grid=(2 * steps,),
         out_shape=[
             jax.ShapeDtypeStruct((ROWS, 2560), F32),
             jax.ShapeDtypeStruct((ROWS, 2560), F32),
@@ -527,8 +526,8 @@
             jax.ShapeDtypeStruct((512, 2560), BF),
         ],
         in_specs=[
-            boxed, boxed, lines, lines, pl.BlockSpec((LINES, 256), lambda i: (i, 0)),
-            pl.BlockSpec((2, 256, HALF), lambda i: (0, 0, 0)), columns,
+            boxed, boxed, lines, lines, pl.BlockSpec((ROWS, 256), lambda i: (0, 0)),
+            pl.BlockSpec((1, 256, WIDTH), lambda i: (i // steps, 0, i % steps)), columns,
         ],
         out_specs=[lines, lines, boxed, columns],
         compiler_params=pltpu.CompilerParams(vmem_limit_bytes=VMEM_MIB * 2**20),

time: 90.7 us -> 91.6 us (level)
  Pallas kernels: 89.7 us -> 90.7 us
    pallas_call x1, Pallas kernels: 9.05 us -> 9.98 us  [body(): pl.pallas_call(finish, name='finish', grid=(2 * steps,), out_shape=[jax.S...]
where the time goes in v5:
time: 91.6 us; the launch traced here: 91.5 us
  Pallas kernels  90.7 us (99%)
    pallas_call x1, Pallas kernels, body(): pl.pallas_call(kernel, name='outer_step', out_shape=[jax.ShapeDtypeStruct...  80.7 us
    pallas_call x1, Pallas kernels, body(): pl.pallas_call(finish, name='finish', grid=(2 * steps,), out_shape=[jax.S...  9.98 us

profile of v5, /device:TPU:1, one launch (start us, length us, event | category | flops | bytes accessed | tf_op | source)
XLA Modules:
  0.0 91.5 jit_solution(337488597601999367)
XLA Ops:
  0.6 80.7 %outer_step.1 = (bf16[320,256]{1,0:T(8,128)(2,1)}, bf16[2,256,1280]{2,1,0:T(8,128)(2,1)}, bf16[512,2560]{1,0:T(8,128)(2,1)}) custom-call(bf16[1,320,2560]{2,1,0:T(8,128)(2,1)} %delta.3, bf16[1,320,2560]{2,1,0:T(8,128)(2,1)} %error.3, f32[320,2560]{1,0:T(8,128)} %params.3, f32[320,2560]{1,0:T(8,128)} %momentum.3, f32[64,2560]{1,0:T(8,128)} %bitcast.1, ...), custom_call_target="tpu_custom_call" | custom-call | flops 15000000512 | bytes 30000000 | tf_op jit(solution)/shard_map/outer_step/pallas_call | solution.py:489
  81.3 10.0 %finish.1 = (f32[320,2560]{1,0:T(8,128)}, f32[320,2560]{1,0:T(8,128)}, bf16[1,320,2560]{2,1,0:T(8,128)(2,1)}, bf16[512,2560]{1,0:T(8,128)(2,1)}) custom-call(bf16[1,320,2560]{2,1,0:T(8,128)(2,1)} %delta.3, bf16[1,320,2560]{2,1,0:T(8,128)(2,1)} %error.3, f32[320,2560]{1,0:T(8,128)} %params.3, f32[320,2560]{1,0:T(8,128)} %momentum.3, ...), custom_call_target="tpu_custom_call" | custom-call | flops 500000000 | bytes 24000000 | tf_op jit(solution)/shard_map/finish/pallas_call | solution.py:518
